TPU v7x, 32 devices: a whole 2x2x4 slice. The times are simulated.
32 devices in a mesh: ctx: 2 (over y), exp: 4 (over z), tp: 4 (over x, core).
Axes of the slice: x: 2, y: 2, z: 4, core: 2. Of those that a mesh axis runs over, the one named last changes fastest.
Arguments:
- queries: bfloat16 [256, 2048], P('ctx', ('exp', 'tp')), may hold values from -30 to 30
- rotated_key_rows: bfloat16 [256, 512], P('ctx', 'exp'), may hold values from -9 to 9
- value_vector_rows: bfloat16 [256, 512], P('ctx', 'exp'), may hold values from -6 to 6
- residual: bfloat16 [256, 4096], P(('ctx', 'exp', 'tp')), may hold values from -6 to 6
- norm_gain: float32 [4096], replicated, may hold values from 0.25 to 1.75
- out_proj: bfloat16 [2048, 4096], P(('exp', 'tp')), may hold values from -0.125 to 0.125
- expert_ids: int32 [256, 2], P('ctx'), may hold values from 0 to 3, all different within a row; in each aligned block of 128 rows (0 to 127, 128 to 255, ...) at most 128 rows name the same one
- gate_weights: float32 [256, 2], P('ctx'), may hold values from 0.2 to 1
- w_gate: bfloat16 [4, 4096, 14336], P('exp', None, ('ctx', 'tp')), may hold values from -0.09375 to 0.09375
- w_up: bfloat16 [4, 4096, 14336], P('exp', None, ('ctx', 'tp')), may hold values from -0.09375 to 0.09375
- w_down: bfloat16 [4, 14336, 4096], P('exp', ('ctx', 'tp')), may hold values from -0.046875 to 0.046875
Outputs:
- mixed: bfloat16 [256, 4096], P(('ctx', 'exp', 'tp'))
Inputs may be any that keep to these rules, and one draw needn't show every extreme that they name: `expert_ids`: each row names 2 different experts. In each aligned block of 128 rows no expert is named by more than 128 rows, and in some block one expert is named by exactly 128 rows.
All inputs are finite; a program needn't handle non-finite values.
Results may differ from a plain program's by a relative error of at most 0.019.
Values may be sent and summed in bfloat16 or wider, within the bound.
A program may use at most 128 MiB of HBM per device.

v0:
```python
import jax
import jax.numpy as jnp
from jax import lax
from jax.sharding import PartitionSpec as P

HEAD_WIDTH = 128


def normalize(hidden_sum, norm_gain):
    mean_square = jnp.mean(hidden_sum * hidden_sum, axis=-1, keepdims=True)
    return (hidden_sum * lax.rsqrt(mean_square + 1e-05) * norm_gain).astype(jnp.bfloat16)


def local(
    queries,
    rotated_key_rows,
    value_vector_rows,
    residual,
    norm_gain,
    out_proj,
    expert_ids,
    gate_weights,
    w_gate,
    w_up,
    w_down,
):
    block_rows = queries.shape[0]
    query_heads = queries.shape[1] // HEAD_WIDTH
    own_rows = residual.shape[0]
    query_first = lax.axis_index("ctx") * block_rows
    query_pos = query_first + jnp.arange(block_rows, dtype=jnp.int32)
    query_view = queries.reshape(block_rows, query_heads, HEAD_WIDTH)
    score_scale = HEAD_WIDTH ** (-0.5)
    row_top = jnp.full((query_heads, block_rows), -1e30, jnp.float32)
    key_piece = lax.all_gather(rotated_key_rows, "ctx", axis=0, tiled=True)
    value_piece = lax.all_gather(value_vector_rows, "ctx", axis=0, tiled=True)
    scores = (
        jnp.einsum("qhd,kd->hqk", query_view, key_piece, preferred_element_type=jnp.float32)
        * score_scale
    )
    key_pos = jnp.arange(key_piece.shape[0], dtype=jnp.int32)
    visible = (key_pos[None, :] <= query_pos[:, None])[None]
    scores = jnp.where(visible, scores, -1e30)
    new_top = jnp.maximum(row_top, jnp.max(scores, axis=2))
    weights = jnp.where(visible, jnp.exp(scores - new_top[..., None]), 0.0)
    row_sum = jnp.sum(weights, axis=2)
    weighted = jnp.einsum(
        "hqk,kd->hqd", weights.astype(jnp.bfloat16), value_piece, preferred_element_type=jnp.float32
    )
    row_top, row_sum, weighted = (new_top, row_sum, weighted)
    attended = (weighted / row_sum[..., None]).astype(jnp.bfloat16)
    attended = jnp.transpose(attended, (1, 0, 2)).reshape(block_rows, query_heads * HEAD_WIDTH)
    share_index = lax.axis_index("exp") * lax.axis_size("tp") + lax.axis_index("tp")
    row_first = share_index * own_rows
    partial_value = jnp.dot(attended, out_proj, preferred_element_type=jnp.float32)
    own_part = lax.dynamic_slice_in_dim(partial_value, row_first, own_rows, 0) + residual.astype(
        jnp.float32
    )
    placed = lax.dynamic_update_slice_in_dim(partial_value, own_part, row_first, 0)
    summed = lax.psum(placed.astype(jnp.bfloat16), ("exp", "tp")).astype(jnp.float32)
    normed_block = normalize(summed, norm_gain)
    own_sum = lax.dynamic_slice_in_dim(summed, row_first, own_rows, 0)
    my_expert = lax.axis_index("exp")
    matches = expert_ids == my_expert
    chosen = jnp.any(matches, axis=1)
    slot_rank = jnp.cumsum(chosen.astype(jnp.int32)) - 1
    gate_share = jnp.sum(jnp.where(matches, gate_weights, 0.0), axis=1)
    capacity = 2 * expert_ids.shape[1] * block_rows // lax.axis_size("exp")
    slot_ids = jnp.arange(capacity, dtype=jnp.int32)
    selector = ((slot_rank[None, :] == slot_ids[:, None]) & chosen[None, :]).astype(jnp.bfloat16)
    picked = jnp.dot(selector, normed_block, preferred_element_type=jnp.float32).astype(
        jnp.bfloat16
    )
    expert_input = lax.all_gather(picked, "ctx", axis=0, tiled=True)
    gate_matrix = w_gate[0]
    up_matrix = w_up[0]
    down_matrix = w_down[0]
    share_rows = capacity // lax.axis_size("tp")
    gate_out = jnp.dot(expert_input, gate_matrix, preferred_element_type=jnp.float32)
    up_out = jnp.dot(expert_input, up_matrix, preferred_element_type=jnp.float32)
    hidden = (jax.nn.silu(gate_out) * up_out).astype(jnp.bfloat16)
    expert_out = lax.psum_scatter(
        jnp.dot(hidden, down_matrix, preferred_element_type=jnp.float32).astype(jnp.bfloat16),
        ("ctx", "tp"),
        scatter_dimension=0,
        tiled=True,
    )
    slot_here = lax.axis_index("tp") * share_rows + jnp.arange(share_rows, dtype=jnp.int32)
    expanded_heads = jnp.where(
        (slot_rank[:, None] == slot_here[None, :]) & chosen[:, None], gate_share[:, None], 0.0
    )
    expert_wide = expert_out.astype(jnp.float32)
    combined = lax.psum_scatter(
        jnp.dot(expanded_heads, expert_wide, precision=lax.Precision.HIGHEST).astype(jnp.bfloat16),
        ("exp", "tp"),
        scatter_dimension=0,
        tiled=True,
    ).astype(jnp.float32)
    return (own_sum + combined).astype(jnp.bfloat16)


def solution(mesh):
    return jax.shard_map(
        local,
        mesh=mesh,
        in_specs=(
            P("ctx", ("exp", "tp")),
            P("ctx", "exp"),
            P("ctx", "exp"),
            P(("ctx", "exp", "tp"), None),
            P(),
            P(("exp", "tp"), None),
            P("ctx", None),
            P("ctx", None),
            P("exp", None, ("ctx", "tp")),
            P("exp", None, ("ctx", "tp")),
            P("exp", ("ctx", "tp"), None),
        ),
        out_specs=P(("ctx", "exp", "tp"), None),
        check_vma=False,
    )
```

profile of v0, /device:TPU:0, one launch (start us, length us, event | category | flops | bytes accessed | tf_op | source)
XLA Modules:
  0.0 286.0 jit_solution(10823428701457201607)
XLA Ops:
  6.5 0.0 copy-start
  6.5 0.0 copy-start.2
  6.5 0.0 all-reduce.2.cloned.1.call-start
  6.5 5.9 %all_gather.9 = bf16[256,128]{1,0:T(8,128)(2,1)S(1)} all-gather(bf16[128,128]{1,0:T(8,128)(2,1)} %param.12), channel_id=1, replica_groups=mesh['ctx'=2,'exp'=4,'tp'=4] {'ctx'}, dimensions={0}, use_global_device_ids=true | all-gather | bytes 98304 | tf_op jit(solution)/shard_map/all_gather | solution.py:35
  12.5 1.0 fusion.50
  13.4 4.8 %all_gather.10 = bf16[256,128]{1,0:T(8,128)(2,1)S(1)} all-gather(bf16[128,128]{1,0:T(8,128)(2,1)} %param.13), channel_id=1, replica_groups=mesh['ctx'=2,'exp'=4,'tp'=4] {'ctx'}, dimensions={0}, use_global_device_ids=true | all-gather | bytes 98304 | tf_op jit(solution)/shard_map/all_gather | solution.py:36
  18.2 0.1 fusion.22
  18.3 0.0 copy-done
  18.3 0.6 fusion.18
  18.9 0.0 copy-done.2
  18.9 0.0 copy-start.4
  18.9 0.0 copy-start.3
  19.0 1.1 convert_element_type.55
  20.1 0.0 all-reduce.2.cloned.1.call-update
  20.1 0.0 all-gather.2.cloned.1.call-start
  20.2 0.0 copy-done.4
  20.2 0.1 copy.13
  20.3 0.2 reduce-window.7
  20.5 0.1 add_reduce_fusion
  20.6 94.5 %all-reduce.2.cloned.1.call-done = bf16[128,4096]{1,0:T(8,128)(2,1)} async-done(((bf16[128,4096]{1,0:T(8,128)(2,1)}), bf16[128,4096]{1,0:T(8,128)(2,1)}) %all-reduce.2.cloned.1.call-update) | async-done | bytes 1048592 | tf_op jit(solution)/shard_map/psum | solution.py:60
  115.1 1.5 multiply_reduce_fusion
  116.6 0.0 copy-done.3
  116.6 2.7 convolution_convert_fusion.1
  119.3 0.0 all-gather.2.cloned.1.call-update
  119.3 0.0 reduce-scatter.3.cloned.1.call-start
  119.4 32.5 %all-gather.2.cloned.1.call-done = bf16[256,4096]{1,0:T(8,128)(2,1)} async-done(((bf16[128,4096]{1,0:T(8,128)(2,1)}), bf16[256,4096]{1,0:T(8,128)(2,1)}) %all-gather.2.cloned.1.call-update) | async-done | bytes 2097168 | tf_op jit(solution)/shard_map/all_gather | solution.py:74
  151.9 0.0 copy-start.6
  151.9 0.0 slice-start
  151.9 0.0 slice-start.1
  151.9 8.5 %fusion.4 = f32[256,1792]{1,0:T(8,128)S(1)} fusion(bf16[256,4096]{1,0:T(8,128)(2,1)} %all-gather.2.cloned.1.call-done, bf16[1,4096,1792]{2,1,0:T(8,128)(2,1)} %param.19), kind=kOutput, calls=%fused_computation.4 | convolution fusion | flops 3758096384 | bytes 18612224 | tf_op jit(solution)/shard_map/dot_general | solution.py:79
  160.4 0.0 copy-done.6
  160.4 0.0 slice-start.2
  160.5 0.0 slice-start.3
  160.5 9.4 %fusion.12 = bf16[256,1792]{1,0:T(8,128)(2,1)S(1)} fusion(bf16[256,4096]{1,0:T(8,128)(2,1)S(1)} %copy-done.6, bf16[1,4096,1792]{2,1,0:T(8,128)(2,1)} %param.20, f32[256,1792]{1,0:T(8,128)S(1)} %fusion.4), kind=kOutput, calls=%fused_computation.10 | convolution fusion | flops 3760848896 | bytes 19529728 | tf_op jit(solution)/shard_map/dot_general | solution.py:80
  169.9 0.0 slice-done
  169.9 0.0 slice-done.1
  169.9 0.0 slice-done.2
  169.9 0.0 slice-done.3
  169.9 5.3 %fusion.6 = bf16[256,4096]{1,0:T(8,128)(2,1)} fusion(bf16[256,1792]{1,0:T(8,128)(2,1)S(1)} %fusion.12, bf16[1,1792,4096]{2,1,0:T(8,128)(2,1)S(1)} %bitcast.36), kind=kOutput, calls=%fused_computation.6 | convolution fusion | flops 3759144960 | bytes 17694720 | tf_op jit(solution)/shard_map/dot_general | solution.py:83
  175.2 0.0 copy-start.5
  175.2 0.0 copy-start.1
  175.2 0.0 reduce-scatter.3.cloned.1.call-update
  175.2 0.0 reduce-scatter.5.cloned.1.call-start
  175.3 0.6 copy-done.5
  175.9 40.7 %reduce-scatter.3.cloned.1.call-done = bf16[32,4096]{1,0:T(8,128)(2,1)} async-done(((bf16[256,4096]{1,0:T(8,128)(2,1)}), bf16[32,4096]{1,0:T(8,128)(2,1)}) %reduce-scatter.3.cloned.1.call-update) | async-done | bytes 262160 | tf_op jit(solution)/shard_map/reduce_scatter | solution.py:82
  216.6 3.0 %convolution_convert_fusion = bf16[128,4096]{1,0:T(8,128)(2,1)} fusion(bf16[32,4096]{1,0:T(8,128)(2,1)} %reduce-scatter.3.cloned.1.call-done, f32[128]{0:T(128)S(1)} %select_reduce_fusion, s32[32]{0:T(128)S(1)} %iota_add_fusion, s32[128]{0:T(128)S(1)} %add_reduce_fusion, pred[128]{0:T(512)(128)(4,1)S(1)} %fusion.49), kind=kOutput, calls=%fused_computation.7 | convolution fusion | flops 201863168 | bytes 1312000 | tf_op jit(solution)/shard_map/dot_general | solution.py:94
  219.6 0.0 reduce-scatter.5.cloned.1.call-update
  219.6 0.0 copy-done.1
  219.6 1.6 convert_element_type.56
  221.2 56.8 %reduce-scatter.5.cloned.1.call-done = bf16[8,4096]{1,0:T(8,128)(2,1)} async-done(((bf16[128,4096]{1,0:T(8,128)(2,1)}), bf16[8,4096]{1,0:T(8,128)(2,1)}) %reduce-scatter.5.cloned.1.call-update) | async-done | bytes 65552 | tf_op jit(solution)/shard_map/reduce_scatter | solution.py:93
  277.9 1.6 add_convert_fusion
  (9 shorter events, 0.1 us)
Async XLA Ops:
  6.5 11.8 %copy-start = (bf16[128,4096]{1,0:T(8,128)(2,1)S(1)}, bf16[128,4096]{1,0:T(8,128)(2,1)}, u32[]{:S(2)}) copy-start(bf16[128,4096]{1,0:T(8,128)(2,1)} %param.16) | copy-start | bytes 3145732
  6.5 12.4 %copy-start.2 = (bf16[8,4096]{1,0:T(8,128)(2,1)S(1)}, bf16[8,4096]{1,0:T(8,128)(2,1)}, u32[]{:S(2)}) copy-start(bf16[8,4096]{1,0:T(8,128)(2,1)} %param.14) | copy-start | bytes 196612
  6.5 108.5 %all-reduce.2.cloned.1.call-start = ((), (), s32[]{:S(2)}) async-start(), calls=%async_computation.2 | async-start | bytes 2097152 | tf_op jit(solution)/shard_map/psum | solution.py:60
  18.9 1.2 copy-start.4
  18.9 97.6 %copy-start.3 = (f32[4096]{0:T(1024)S(1)}, f32[4096]{0:T(1024)}, u32[]{:S(2)}) copy-start(f32[4096]{0:T(1024)} %param.15) | copy-start | bytes 49156
  20.1 131.8 %all-gather.2.cloned.1.call-start = ((), (), s32[]{:S(2)}) async-start(), calls=%async_computation.3 | async-start | bytes 3145728 | tf_op jit(solution)/shard_map/all_gather | solution.py:74
  119.3 97.3 %reduce-scatter.3.cloned.1.call-start = ((), (), s32[]{:S(2)}) async-start(), calls=%async_computation.4 | async-start | bytes 2359296 | tf_op jit(solution)/shard_map/reduce_scatter | solution.py:82
  151.9 8.6 %copy-start.6 = (bf16[256,4096]{1,0:T(8,128)(2,1)S(1)}, bf16[256,4096]{1,0:T(8,128)(2,1)}, u32[]{:S(2)}) copy-start(bf16[256,4096]{1,0:T(8,128)(2,1)} %all-gather.2.cloned.1.call-done) | copy-start | bytes 6291460
  151.9 18.0 %slice-start = ((s8[14680064]{0:T(1024)(128)(4,1)}), s8[4194304]{0:T(1024)(128)(4,1)S(1)}, s32[]{:S(2)}) async-start(s8[14680064]{0:T(1024)(128)(4,1)} %bitcast.35), calls=%async_computation.6 | async-start | bytes 8388608
  151.9 18.0 %slice-start.1 = ((s8[14680064]{0:T(1024)(128)(4,1)}), s8[4194304]{0:T(1024)(128)(4,1)S(1)}, s32[]{:S(2)}) async-start(s8[14680064]{0:T(1024)(128)(4,1)} %bitcast.35), calls=%async_computation.7 | async-start | bytes 8388608
  160.4 9.5 %slice-start.2 = ((s8[14680064]{0:T(1024)(128)(4,1)}), s8[4194304]{0:T(1024)(128)(4,1)S(1)}, s32[]{:S(2)}) async-start(s8[14680064]{0:T(1024)(128)(4,1)} %bitcast.35), calls=%async_computation.8 | async-start | bytes 8388608
  160.5 9.5 %slice-start.3 = ((s8[14680064]{0:T(1024)(128)(4,1)}), s8[2097152]{0:T(1024)(128)(4,1)S(1)}, s32[]{:S(2)}) async-start(s8[14680064]{0:T(1024)(128)(4,1)} %bitcast.35), calls=%async_computation.9 | async-start | bytes 4194304
  175.2 0.7 copy-start.5
  175.2 44.4 %copy-start.1 = (bf16[128,4096]{1,0:T(8,128)(2,1)S(1)}, bf16[128,4096]{1,0:T(8,128)(2,1)}, u32[]{:S(2)}) copy-start(bf16[128,4096]{1,0:T(8,128)(2,1)} %all-reduce.2.cloned.1.call-done) | copy-start | bytes 3145732
  175.2 102.7 %reduce-scatter.5.cloned.1.call-start = ((), (), s32[]{:S(2)}) async-start(), calls=%async_computation.5 | async-start | bytes 1114112 | tf_op jit(solution)/shard_map/reduce_scatter | solution.py:93
Sparse Core Ops, SparseCore 0:
  20.2 94.7 all-reduce.1
  119.5 32.3 all-gather.1
  175.3 41.2 reduce-scatter.2
  220.5 57.3 reduce-scatter.4
where the time goes:
time: 286 us
  waiting for transfers between devices  224 us (78%)
  matrix products  30.4 us (11%)
  between operations  13.3 us (5%)
  blocking collectives  10.7 us (4%)
  other arithmetic  6.21 us (2%)
    psum x1, waiting for transfers between devices, local(): lax.psum(placed.astype(jnp.bfloat16), ('exp', 'tp')).astype(jnp.float32)  94.5 us
    reduce_scatter x1, waiting for transfers between devices, local(): lax.psum_scatter(jnp.dot(expanded_heads, expert_wide, precision=lax.Preci...  56.8 us
    reduce_scatter x1, waiting for transfers between devices, local(): lax.psum_scatter(jnp.dot(hidden, down_matrix, preferred_element_type=jnp....  40.7 us
    all_gather x1, waiting for transfers between devices, local(): expert_input = lax.all_gather(picked, 'ctx', axis=0, tiled=True)  32.5 us
    dot_general x1, matrix products, local(): jnp.dot(expert_input, up_matrix, preferred_element_type=jnp.float32)  9.41 us
    dot_general x1, matrix products, local(): jnp.dot(expert_input, gate_matrix, preferred_element_type=jnp.float32)  8.54 us
    all_gather x1, blocking collectives, local(): key_piece = lax.all_gather(rotated_key_rows, 'ctx', axis=0, tiled=True)  5.92 us
  transfers between devices with their start and end apart: 4, of which 4 were waited for; matrix products, arithmetic and copies ran while one was open for 1% of the time, Pallas kernels for 0%

commit v1 on v0

--- a/solution.py
+++ b/solution.py
@@ -1,6 +1,11 @@
+import functools
+import math
+
 import jax
 import jax.numpy as jnp
 from jax import lax
+from jax.experimental import pallas as pl
+from jax.experimental.pallas import tpu as pltpu
 from jax.sharding import PartitionSpec as P
 
 HEAD_WIDTH = 128
@@ -11,7 +16,7 @@
     return (hidden_sum * lax.rsqrt(mean_square + 1e-05) * norm_gain).astype(jnp.bfloat16)
 
 
-def local(
+def local_collectives(
     queries,
     rotated_key_rows,
     value_vector_rows,
@@ -63,7 +68,9 @@
     my_expert = lax.axis_index("exp")
     matches = expert_ids == my_expert
     chosen = jnp.any(matches, axis=1)
-    slot_rank = jnp.cumsum(chosen.astype(jnp.int32)) - 1
+    order = jnp.arange(block_rows, dtype=jnp.int32)
+    before = (order[None, :] <= order[:, None]) & chosen[None, :]
+    slot_rank = jnp.sum(before.astype(jnp.int32), axis=1) - 1
     gate_share = jnp.sum(jnp.where(matches, gate_weights, 0.0), axis=1)
     capacity = 2 * expert_ids.shape[1] * block_rows // lax.axis_size("exp")
     slot_ids = jnp.arange(capacity, dtype=jnp.int32)
@@ -99,9 +106,308 @@
     return (own_sum + combined).astype(jnp.bfloat16)
 
 
+CHUNKS = 4
+TILE = 256
+MESH = pl.DeviceIdType.MESH
+F32 = jnp.float32
+BF16 = jnp.bfloat16
+
+
+def pack(low, high):
+    blocks = low.shape[0] // 8
+    low = low.reshape(blocks, 8, low.shape[1])
+    high = high.reshape(blocks, 8, high.shape[1])
+    return jnp.concatenate([low, high], axis=1)
+
+
+def layer_kernel(sizes, q_ref, k_ref, v_ref, res_ref, gain_ref, proj_ref, gate_ref, wg_hbm, wu_hbm, wd_hbm, out_ref,
+                 wg, wu, wd, k_all, v_all, att, p1, p1_core, s1, s1_x, s2, s2_z, h, xg, xs, hid,
+                 p2, p2_core, t1, t1_x, t2a, t1_y, t2b, t2a_y, t2b_x, t3, t3_z,
+                 w_sem, send_sem, recv_sem):
+    C, E, X, K = sizes
+    rows = q_ref.shape[0]
+    width = p1.shape[-1]
+    half = width * CHUNKS
+    ctx, exp, tp = lax.axis_index("ctx"), lax.axis_index("exp"), lax.axis_index("tp")
+    x, core = lax.div(tp, K), lax.rem(tp, K)
+    groups = {
+        "ctx": ("ctx", ctx, 1, C, ctx),
+        "exp": ("exp", exp, 1, E, exp),
+        "x": ("tp", tp, K, X, x),
+        "core": ("tp", tp, 1, K, core),
+    }
+
+    weights = [
+        pltpu.make_async_copy(wg_hbm.at[0], wg, w_sem.at[0]),
+        pltpu.make_async_copy(wu_hbm.at[0], wu, w_sem.at[1]),
+        pltpu.make_async_copy(wd_hbm.at[0], wd, w_sem.at[2]),
+    ]
+
+    def partner(group, offset):
+        axis, index, stride, members, digit = groups[group]
+        other = lax.rem(digit + offset, members)
+        return other, {axis: index + (other - digit) * stride}
+
+    barrier = pltpu.get_barrier_semaphore()
+    greeted = 0
+    for group in groups:
+        for offset in range(1, groups[group][3]):
+            _, device = partner(group, offset)
+            pl.semaphore_signal(barrier, inc=1, device_id=device, device_id_type=MESH)
+            greeted += 1
+    for copy in weights:
+        copy.start()
+    pl.semaphore_wait(barrier, greeted)
+
+    used = [0]
+    sent = []
+
+    def exchange(group, source, target):
+        copies = []
+        for offset in range(1, groups[group][3]):
+            other, device = partner(group, offset)
+            copy = pltpu.make_async_remote_copy(
+                src_ref=source(other),
+                dst_ref=target(offset - 1),
+                send_sem=send_sem.at[used[0]],
+                recv_sem=recv_sem.at[used[0]],
+                device_id=device,
+                device_id_type=MESH,
+            )
+            used[0] += 1
+            copy.start()
+            copies.append(copy)
+            sent.append(copy)
+        return copies
+
+    def arrived(copies):
+        for copy in copies:
+            copy.wait_recv()
+
+    def total(own, slots):
+        value = own[...].astype(F32)
+        for i in range(slots.shape[0]):
+            value = value + slots[i].astype(F32)
+        return value
+
+    chunks = range(CHUNKS)
+
+    k_all[ctx] = k_ref[...]
+    v_all[ctx] = v_ref[...]
+    pending = exchange("ctx", lambda j: k_all.at[ctx], lambda i: k_all.at[ctx])
+    pending += exchange("ctx", lambda j: v_all.at[ctx], lambda i: v_all.at[ctx])
+    arrived(pending)
+
+    keys = k_all[...].reshape(C * rows, HEAD_WIDTH)
+    values = v_all[...].reshape(C * rows, HEAD_WIDTH)
+    query_pos = ctx * rows + lax.broadcasted_iota(jnp.int32, (rows, C * rows), 0)
+    visible = lax.broadcasted_iota(jnp.int32, (rows, C * rows), 1) <= query_pos
+    for head in range(q_ref.shape[1] // HEAD_WIDTH):
+        columns = slice(head * HEAD_WIDTH, (head + 1) * HEAD_WIDTH)
+        scores = lax.dot_general(
+            q_ref[:, columns], keys, (((1,), (1,)), ((), ())), preferred_element_type=F32
+        ) * HEAD_WIDTH ** (-0.5)
+        scores = jnp.where(visible, scores, -1e30)
+        top = jnp.max(scores, axis=1, keepdims=True)
+        weight = jnp.where(visible, jnp.exp(scores - top), 0.0)
+        row_sum = jnp.sum(weight, axis=1, keepdims=True)
+        weighted = jnp.dot(weight.astype(BF16), values, preferred_element_type=F32)
+        att[:, columns] = (weighted / row_sum).astype(BF16)
+
+    flight = []
+    for ch in chunks:
+        low = slice(ch * width, (ch + 1) * width)
+        high = slice(half + ch * width, half + (ch + 1) * width)
+        part = pack(
+            jnp.dot(att[...], proj_ref[:, low], preferred_element_type=F32),
+            jnp.dot(att[...], proj_ref[:, high], preferred_element_type=F32),
+        )
+        p1[ch] = part.astype(BF16).reshape(E, X, K, 16, width)
+        flight.append(exchange("core", lambda j: p1.at[ch, :, :, j], lambda i: p1_core.at[ch, i]))
+    for ch in chunks:
+        arrived(flight[ch])
+        s1[ch] = total(p1.at[ch, :, :, core], p1_core.at[ch]).astype(BF16)
+        flight[ch] = exchange("x", lambda j: s1.at[ch, :, j], lambda i: s1_x.at[ch, i])
+    for ch in chunks:
+        arrived(flight[ch])
+        s2[ch] = total(s1.at[ch, :, x], s1_x.at[ch]).astype(BF16)
+        flight[ch] = exchange("exp", lambda j: s2.at[ch, j], lambda i: s2_z.at[ch, i])
+    square = jnp.zeros((8, 1), F32)
+    for ch in chunks:
+        low = slice(ch * width, (ch + 1) * width)
+        high = slice(half + ch * width, half + (ch + 1) * width)
+        arrived(flight[ch])
+        residual = jnp.concatenate([res_ref[:, low].astype(F32), res_ref[:, high].astype(F32)], axis=0)
+        value = total(s2.at[ch, exp], s2_z.at[ch]) + residual
+        h[ch] = value
+        both = jnp.sum(value * value, axis=1, keepdims=True)
+        square = square + both[:8] + both[8:]
+    scale = lax.rsqrt(square / (2 * half) + 1e-05)
+    scale = jnp.concatenate([scale, scale], axis=0)
+
+    for ch in chunks:
+        low = slice(ch * width, (ch + 1) * width)
+        high = slice(half + ch * width, half + (ch + 1) * width)
+        gain = jnp.concatenate(
+            [jnp.broadcast_to(gain_ref[:, low], (8, width)), jnp.broadcast_to(gain_ref[:, high], (8, width))], axis=0
+        )
+        xg[ch, ctx, exp, x, core] = (h[ch] * scale * gain).astype(BF16)
+        own = xg.at[ch, ctx, exp, x, core]
+        flight[ch] = exchange("exp", lambda j: own, lambda i: own)
+    for ch in chunks:
+        arrived(flight[ch])
+        own = xg.at[ch, ctx, :, x, core]
+        flight[ch] = exchange("x" if ch % 2 else "ctx", lambda j: own, lambda i: own)
+    for ch in chunks:
+        arrived(flight[ch])
+        own = xg.at[ch, ctx, :, :, core] if ch % 2 else xg.at[ch, :, :, x, core]
+        flight[ch] = exchange("ctx" if ch % 2 else "x", lambda j: own, lambda i: own)
+    for ch in chunks:
+        arrived(flight[ch])
+        own = xg.at[ch, :, :, :, core]
+        flight[ch] = exchange("core", lambda j: own, lambda i: own)
+    every = C * rows
+    for ch in chunks:
+        arrived(flight[ch])
+        block = xg[ch].reshape(every // 8, 16, width).astype(F32)
+        xs[:, ch * width : (ch + 1) * width] = block[:, :8].reshape(every, width).astype(BF16)
+        xs[:, half + ch * width : half + (ch + 1) * width] = block[:, 8:].reshape(every, width).astype(BF16)
+
+    weights[0].wait()
+    weights[1].wait()
+
+    @pl.loop(0, hid.shape[1] // TILE)
+    def _(j):
+        columns = pl.ds(pl.multiple_of(j * TILE, TILE), TILE)
+        gate = jnp.dot(xs[...], wg[:, columns], preferred_element_type=F32)
+        up = jnp.dot(xs[...], wu[:, columns], preferred_element_type=F32)
+        hid[:, columns] = (gate / (1.0 + jnp.exp(-gate)) * up).astype(BF16)
+
+    weights[2].wait()
+
+    def after_core(ch):
+        arrived(flight[ch])
+        t1[ch] = total(p2.at[ch, :, :, :, core], p2_core.at[ch]).astype(BF16)
+        if ch % 2:
+            flight[ch] = exchange("ctx", lambda j: t1.at[ch, j], lambda i: t1_y.at[ch, i])
+        else:
+            flight[ch] = exchange("x", lambda j: t1.at[ch, :, :, j], lambda i: t1_x.at[ch, i])
+
+    for ch in chunks:
+
+        @pl.loop(0, width // TILE)
+        def _(j):
+            low = pl.ds(pl.multiple_of(ch * width + j * TILE, TILE), TILE)
+            high = pl.ds(pl.multiple_of(half + ch * width + j * TILE, TILE), TILE)
+            part = pack(
+                jnp.dot(hid[...], wd[:, low], preferred_element_type=F32),
+                jnp.dot(hid[...], wd[:, high], preferred_element_type=F32),
+            )
+            p2[ch, :, :, :, :, :, pl.ds(pl.multiple_of(j * TILE, TILE), TILE)] = part.astype(BF16).reshape(
+                C, E, X, K, 16, TILE
+            )
+
+        flight[ch] = exchange("core", lambda j: p2.at[ch, :, :, :, j], lambda i: p2_core.at[ch, i])
+        if ch:
+            after_core(ch - 1)
+    after_core(CHUNKS - 1)
+    for ch in chunks:
+        arrived(flight[ch])
+        if ch % 2:
+            t2b[ch] = total(t1.at[ch, ctx], t1_y.at[ch]).astype(BF16)
+            flight[ch] = exchange("x", lambda j: t2b.at[ch, :, j], lambda i: t2b_x.at[ch, i])
+        else:
+            t2a[ch] = total(t1.at[ch, :, :, x], t1_x.at[ch]).astype(BF16)
+            flight[ch] = exchange("ctx", lambda j: t2a.at[ch, j], lambda i: t2a_y.at[ch, i])
+    for ch in chunks:
+        arrived(flight[ch])
+        if ch % 2:
+            value = total(t2b.at[ch, :, x], t2b_x.at[ch])
+        else:
+            value = total(t2a.at[ch, ctx], t2a_y.at[ch])
+        t3[ch] = (value * gate_ref[...]).astype(BF16)
+        flight[ch] = exchange("exp", lambda j: t3.at[ch, j], lambda i: t3_z.at[ch, i])
+    for ch in chunks:
+        arrived(flight[ch])
+        value = (total(t3.at[ch, exp], t3_z.at[ch]) + h[ch]).astype(BF16).astype(F32)
+        out_ref[:, ch * width : (ch + 1) * width] = value[:8].astype(BF16)
+        out_ref[:, half + ch * width : half + (ch + 1) * width] = value[8:].astype(BF16)
+    for copy in sent:
+        copy.wait_send()
+
+
+def local(shape, *args):
+    queries, keys, values, residual, norm_gain, out_proj, expert_ids, gate_weights, w_gate, w_up, w_down = args
+    C, E, T = shape["ctx"], shape["exp"], shape["tp"]
+    rows, model = queries.shape[0], residual.shape[1]
+    capacity = 2 * expert_ids.shape[1] * rows // E
+    if capacity < rows or T % 2 or residual.shape[0] != 8 or keys.shape[1] != HEAD_WIDTH:
+        return local_collectives(*args)
+    K, X = 2, T // 2
+    hidden = w_gate.shape[2]
+    width = model // 2 // CHUNKS
+
+    share = jnp.sum(jnp.where(expert_ids == lax.axis_index("exp"), gate_weights, 0.0), axis=1)
+    share = lax.dynamic_index_in_dim(share.reshape(E, T, 8), lax.axis_index("tp"), 1, keepdims=False)
+    share = jnp.concatenate([share, share], axis=1)[:, :, None]
+
+    vmem = pl.BlockSpec(memory_space=pltpu.VMEM)
+    hbm = pl.BlockSpec(memory_space=pl.ANY)
+    copies = 2 * (C - 1) + CHUNKS * (3 * (K - 1) + 3 * (X - 1) + 3 * (E - 1) + 2 * (C - 1))
+
+    def buffer(*dims, dtype=BF16):
+        return pltpu.VMEM(dims, dtype)
+
+    tile = (16, width)
+    return pl.pallas_call(
+        functools.partial(layer_kernel, (C, E, X, K)),
+        out_shape=jax.ShapeDtypeStruct((residual.shape[0], model), BF16),
+        in_specs=[vmem] * 7 + [hbm] * 3,
+        out_specs=vmem,
+        scratch_shapes=[
+            buffer(model, hidden),
+            buffer(model, hidden),
+            buffer(hidden, model),
+            buffer(C, rows, HEAD_WIDTH),
+            buffer(C, rows, HEAD_WIDTH),
+            buffer(*queries.shape),
+            buffer(CHUNKS, E, X, K, *tile),
+            buffer(CHUNKS, K - 1, E, X, *tile),
+            buffer(CHUNKS, E, X, *tile),
+            buffer(CHUNKS, X - 1, E, *tile),
+            buffer(CHUNKS, E, *tile),
+            buffer(CHUNKS, E - 1, *tile),
+            buffer(CHUNKS, *tile, dtype=F32),
+            buffer(CHUNKS, C, E, X, K, *tile),
+            buffer(C * rows, model),
+            buffer(C * rows, hidden),
+            buffer(CHUNKS, C, E, X, K, *tile),
+            buffer(CHUNKS, K - 1, C, E, X, *tile),
+            buffer(CHUNKS, C, E, X, *tile),
+            buffer(CHUNKS, X - 1, C, E, *tile),
+            buffer(CHUNKS, C, E, *tile),
+            buffer(CHUNKS, C - 1, E, X, *tile),
+            buffer(CHUNKS, E, X, *tile),
+            buffer(CHUNKS, C - 1, E, *tile),
+            buffer(CHUNKS, X - 1, E, *tile),
+            buffer(CHUNKS, E, *tile),
+            buffer(CHUNKS, E - 1, *tile),
+            pltpu.SemaphoreType.DMA((3,)),
+            pltpu.SemaphoreType.DMA((copies,)),
+            pltpu.SemaphoreType.DMA((copies,)),
+        ],
+        compiler_params=pltpu.CompilerParams(
+            collective_id=0, has_side_effects=True, vmem_limit_bytes=62 * 1024 * 1024
+        ),
+        cost_estimate=pl.CostEstimate(
+            flops=6 * C * rows * model * hidden, bytes_accessed=6 * model * hidden, transcendentals=C * rows * hidden
+        ),
+    )(queries, keys, values, residual, norm_gain.reshape(1, model), out_proj, share, w_gate, w_up, w_down)
+
+
 def solution(mesh):
     return jax.shard_map(
-        local,
+        functools.partial(local, dict(mesh.shape)),
         mesh=mesh,
         in_specs=(
             P("ctx", ("exp", "tp")),

time: 286 us -> 74.4 us (0.26)
  waiting for transfers between devices: 224 us -> 0 us
  Pallas kernels: 0 us -> 71.1 us
  matrix products: 30.4 us -> 0 us
  between operations: 13.3 us -> 0.02 us
  blocking collectives: 10.7 us -> 0 us
  other arithmetic: 6.21 us -> 0.79 us
    reduce_scatter x2 -> x0, waiting for transfers between devices: 97.5 us -> none  [the longest x1 56.8 us: local(): lax.psum_scatter(jnp.dot(expanded_heads, expert_wide, precision=lax.Preci...]
    psum x1 -> x0, waiting for transfers between devices: 94.5 us -> none  [local(): lax.psum(placed.astype(jnp.bfloat16), ('exp', 'tp')).astype(jnp.float32)]
    pallas_call x0 -> x1, Pallas kernels: none -> 71.1 us  [local(): pl.pallas_call(functools.partial(layer_kernel, (C, E, X, K)), out_shape=j...]
    all_gather x1 -> x0, waiting for transfers between devices: 32.5 us -> none  [local(): expert_input = lax.all_gather(picked, 'ctx', axis=0, tiled=True)]
    dot_general x7 -> x0, matrix products: 30.4 us -> none  [the longest x1 9.41 us: local(): jnp.dot(expert_input, up_matrix, preferred_element_type=jnp.float32)]
    all_gather x2 -> x0, blocking collectives: 10.7 us -> none  [the longest x1 5.92 us: local(): key_piece = lax.all_gather(rotated_key_rows, 'ctx', axis=0, tiled=True)]
    convert_element_type x4 -> x0, other arithmetic: 4.27 us -> none  [the longest x1 1.59 us: local(): return (own_sum + combined).astype(jnp.bfloat16)]
  transfers between devices with their start and end apart: 4 -> 0, of which waited for: 4 -> 0; matrix products, arithmetic and copies ran while one was open for 1% -> 0% of each run, Pallas kernels for 0% -> 0%
where the time goes in v1:
time: 74.4 us; the launch traced here: 74.2 us
  Pallas kernels  71.1 us (96%)
  local copies, waits for them, and re-layouts  2.3 us (3%)
  other arithmetic  0.79 us (1%)
    pallas_call x1, Pallas kernels, local(): pl.pallas_call(functools.partial(layer_kernel, (C, E, X, K)), out_shape=j...  71.1 us

profile of v1, /device:TPU:0, one launch (start us, length us, event | category | flops | bytes accessed | tf_op | source)
XLA Modules:
  0.0 74.2 jit_solution(1148413328202407068)
XLA Ops:
  0.0 0.7 fusion
  0.7 0.1 reshape.7
  0.8 0.1 maximum_bitcast_fusion
  0.9 0.7 copy.12.gate_ref
  1.6 71.1 %shard_map.109 = bf16[8,4096]{1,0:T(8,128)(2,1)} custom-call(bf16[128,128]{1,0:T(8,128)(2,1)} %q_ref.1, bf16[128,128]{1,0:T(8,128)(2,1)} %k_ref.1, bf16[128,128]{1,0:T(8,128)(2,1)} %v_ref.1, bf16[8,4096]{1,0:T(8,128)(2,1)} %res_ref.1, f32[1,4096]{1,0:T(1,128)} %bitcast.4, bf16[128,4096]{1,0:T(8,128)(2,1)} %proj_ref.1, f32[4,16,1]{2,1,0:T(8,128)} %copy.12.gate_ref, ...), custom_call_target="tpu_custom_call" | custom-call | flops 11274289152 | bytes 44040192 | tf_op jit(solution)/shard_map/pallas_call | solution.py:362
  72.7 1.5 %copy.14 = bf16[8,4096]{1,0:T(8,128)(2,1)} copy(bf16[8,4096]{1,0:T(8,128)(2,1)} %shard_map.109) | data formatting | bytes 131072
  (1 shorter events, 0.0 us)

commit v2 on v1

--- a/solution.py
+++ b/solution.py
@@ -106,7 +106,7 @@
     return (own_sum + combined).astype(jnp.bfloat16)
 
 
-CHUNKS = 4
+CHUNKS = 8
 TILE = 256
 MESH = pl.DeviceIdType.MESH
 F32 = jnp.float32

time: 74.4 us -> 73.9 us (level)
  no operation moved by 1% of the time
where the time goes in v2:
time: 73.9 us; the launch traced here: 73.7 us
  Pallas kernels  70.6 us (96%)
  local copies, waits for them, and re-layouts  2.3 us (3%)
  other arithmetic  0.79 us (1%)
    pallas_call x1, Pallas kernels, local(): pl.pallas_call(functools.partial(layer_kernel, (C, E, X, K)), out_shape=j...  70.6 us

profile of v2, /device:TPU:0, one launch (start us, length us, event | category | flops | bytes accessed | tf_op | source)
XLA Modules:
  0.0 73.7 jit_solution(17492262953378101398)
XLA Ops:
  0.0 0.7 fusion
  0.7 0.1 reshape.7
  0.8 0.1 maximum_bitcast_fusion
  0.9 0.7 copy.12.gate_ref
  1.6 70.6 %shard_map.109 = bf16[8,4096]{1,0:T(8,128)(2,1)} custom-call(bf16[128,128]{1,0:T(8,128)(2,1)} %q_ref.1, bf16[128,128]{1,0:T(8,128)(2,1)} %k_ref.1, bf16[128,128]{1,0:T(8,128)(2,1)} %v_ref.1, bf16[8,4096]{1,0:T(8,128)(2,1)} %res_ref.1, f32[1,4096]{1,0:T(1,128)} %bitcast.4, bf16[128,4096]{1,0:T(8,128)(2,1)} %proj_ref.1, f32[4,16,1]{2,1,0:T(8,128)} %copy.12.gate_ref, ...), custom_call_target="tpu_custom_call" | custom-call | flops 11274289152 | bytes 44040192 | tf_op jit(solution)/shard_map/pallas_call | solution.py:362
  72.2 1.5 %copy.14 = bf16[8,4096]{1,0:T(8,128)(2,1)} copy(bf16[8,4096]{1,0:T(8,128)(2,1)} %shard_map.109) | data formatting | bytes 131072
  (1 shorter events, 0.0 us)
